TPU v7x, 32 devices: a whole 2x2x4 slice. The times are simulated.
32 devices in a mesh: group: 2 (over x), ctx: 16 (over z, y, core).
Axes of the slice: x: 2, y: 2, z: 4, core: 2. Of those that a mesh axis runs over, the one named last changes fastest.
Arguments:
- normed_hidden: bfloat16 [4096, 8192], P(('group', 'ctx')), parts along dimension 0, may hold values from -6 to 6
- queries: bfloat16 [4096, 4096], P(('group', 'ctx')), parts along dimension 0, may hold values from -45 to 45
- keys: bfloat16 [4096, 512], P(('group', 'ctx')), parts along dimension 0, may hold values from -6 to 6
- value_frozen_matrix: bfloat16 [8192, 512], P('ctx'), may hold values from -0.0625 to 0.0625
- adapter_down_weight: bfloat16 [8192, 64], replicated, may hold values from -0.0625 to 0.0625
- adapter_up_weight: bfloat16 [64, 512], replicated, may hold values from -0.75 to 0.75
- block_slot_index: int32 [64], P(('group', 'ctx')), parts along dimension 0, may hold values from 0 to 31, each once
Outputs:
- attended: bfloat16 [4096, 4096], P(('group', 'ctx')), parts along dimension 0
There are 2 independent parts, one for each index of `group`. A program takes and returns all parts, laid end to end along the dimension named above; an argument that names none is the same for every part. Nothing has to cross between parts.
Inputs may be any that keep to these rules, and one draw needn't show every extreme that they name: `block_slot_index`: each of the 32 blocks is named once; slot j holds rows j*64 to (j+1)*64 - 1.
All inputs are finite; a program needn't handle non-finite values.
Results may differ from a plain program's by a relative error of at most 0.0054.
Values may be sent and summed in bfloat16 or wider, within the bound.
A program may use at most 192 MiB of HBM per device.

v0:
```python
import jax
import jax.numpy as jnp
from jax import lax
from jax.sharding import PartitionSpec as P

QH = 32
KVH = 4
HD = 128
BLK = 64


def shards(
    normed_hidden,
    queries,
    keys,
    value_frozen_matrix,
    adapter_down_weight,
    adapter_up_weight,
    block_slot_index,
):
    tokens = normed_hidden.shape[0]
    scale = 1.0 / HD**0.5
    offsets = jnp.arange(BLK, dtype=jnp.int32)
    table = lax.all_gather(block_slot_index, "ctx", axis=0, tiled=True)
    my_pos = (block_slot_index[:, None] * BLK + offsets[None, :]).reshape(tokens)
    frozen_output = jnp.dot(
        normed_hidden,
        lax.all_gather(value_frozen_matrix, "ctx", axis=0, tiled=True),
        preferred_element_type=jnp.float32,
    )
    low_rank_output = jnp.dot(
        normed_hidden, adapter_down_weight, preferred_element_type=jnp.float32
    ).astype(jnp.bfloat16)
    value_output = (
        frozen_output
        + 0.5 * jnp.dot(low_rank_output, adapter_up_weight, preferred_element_type=jnp.float32)
    ).astype(jnp.bfloat16)
    slots_here = tokens // BLK
    query_slots = [
        queries[which * BLK : (which + 1) * BLK].reshape(BLK, KVH, QH // KVH, HD)
        for which in range(slots_here)
    ]
    pos_slots = [my_pos[which * BLK : (which + 1) * BLK] for which in range(slots_here)]
    shape_stat = (KVH, QH // KVH, BLK)
    init = tuple(
        (
            (
                jnp.full(shape_stat, -1e30, jnp.float32),
                jnp.zeros(shape_stat, jnp.float32),
                jnp.zeros(shape_stat + (HD,), jnp.float32),
            )
            for which in range(slots_here)
        )
    )
    key_piece = lax.all_gather(keys, "ctx", axis=0, tiled=True)
    count = key_piece.shape[0]
    key_pos = (table[:, None] * BLK + offsets[None, :]).reshape(count)
    key_three = key_piece.reshape(count, KVH, HD)
    value_three = lax.all_gather(value_output, "ctx", axis=0, tiled=True).reshape(count, KVH, HD)
    lowest_key = jnp.min(key_pos)
    updated = []
    for attend_which in range(slots_here):
        q_part = query_slots[attend_which]
        q_pos = pos_slots[attend_which]

        def update(state, q_part=q_part, q_pos=q_pos):
            top, total, accum = state
            scores = (
                jnp.einsum("tkgd,skd->kgts", q_part, key_three, preferred_element_type=jnp.float32)
                * scale
            )
            visible = (q_pos[:, None] >= key_pos[None, :])[None, None]
            scores = jnp.where(visible, scores, -1e30)
            top_new = jnp.maximum(top, jnp.max(scores, axis=-1))
            weights = jnp.where(visible, jnp.exp(scores - top_new[..., None]), 0.0)
            total = jnp.sum(weights, axis=-1)
            accum = jnp.einsum(
                "kgts,skd->kgtd",
                weights.astype(jnp.bfloat16),
                value_three,
                preferred_element_type=jnp.float32,
            )
            return (top_new, total, accum)

        def keep(state):
            return state

        updated.append(lax.cond(lowest_key <= jnp.max(q_pos), update, keep, init[attend_which]))
    states = tuple(updated)
    outputs = []
    for which in range(slots_here):
        result = states[which][2] / states[which][1][..., None]
        outputs.append(
            jnp.transpose(result, (2, 0, 1, 3)).reshape(BLK, QH * HD).astype(jnp.bfloat16)
        )
    return jnp.concatenate(outputs, axis=0)


def solution(mesh):
    in_specs = (
        P(("group", "ctx"), None),
        P(("group", "ctx"), None),
        P(("group", "ctx"), None),
        P("ctx", None),
        P(),
        P(),
        P(("group", "ctx")),
    )
    out_specs = P(("group", "ctx"), None)
    return jax.shard_map(shards, mesh=mesh, in_specs=in_specs, out_specs=out_specs, check_vma=False)
```

profile of v0, /device:TPU:0, one launch (start us, length us, event | category | flops | bytes accessed | tf_op | source)
XLA Modules:
  0.0 217.2 jit_solution(570349210918793714)
XLA Ops:
  6.5 0.0 copy-start
  6.5 0.0 all-gather.6.cloned.1.call-start
  6.6 0.7 all-gather.6.cloned.1.call-update
  7.3 0.0 all-gather.8.cloned.1.call-start
  7.3 79.8 %all-gather.6.cloned.1.call-done = bf16[8192,512]{1,0:T(8,128)(2,1)} async-done(((bf16[512,512]{1,0:T(8,128)(2,1)}), bf16[8192,512]{1,0:T(8,128)(2,1)}) %all-gather.6.cloned.1.call-update) | async-done | bytes 8388624 | tf_op jit(solution)/shard_map/all_gather | solution.py:28
  87.2 0.0 copy-done
  87.2 4.6 %fusion.31 = f32[128,512]{1,0:T(8,128)S(1)} fusion(bf16[128,8192]{1,0:T(8,128)(2,1)S(1)} %copy-done, bf16[8192,512]{1,0:T(8,128)(2,1)} %all-gather.6.cloned.1.call-done), kind=kOutput, calls=%fused_computation.52 | convolution fusion | flops 1073741824 | bytes 10747904 | tf_op jit(solution)/shard_map/dot_general | solution.py:26
  91.8 0.0 copy-done.3
  91.8 2.4 %fusion.27 = bf16[128,512]{1,0:T(8,128)(2,1)} fusion(f32[128,512]{1,0:T(8,128)S(1)} %fusion.31, bf16[64,512]{1,0:T(8,128)(2,1)} %param.16, bf16[128,8192]{1,0:T(8,128)(2,1)S(1)} %copy-done, bf16[8192,64]{0,1:T(8,128)(2,1)S(1)} %copy-done.3), kind=kOutput, calls=%fused_computation.36 | convolution fusion | flops 142811136 | bytes 3604480 | tf_op jit(solution)/shard_map/dot_general | solution.py:36
  94.2 0.0 all-gather.8.cloned.1.call-update
  94.2 0.0 all-gather.4.cloned.1.call-start
  94.3 0.0 copy-done.4
  94.3 0.8 copy.14
  95.0 0.0 all-gather.4.cloned.1.call-update
  95.1 0.0 copy-done.6
  95.1 0.6 dynamic-slice
  96.2 0.0 copy-done.5
  96.2 0.2 dynamic-update-slice
  96.5 9.6 %all-reduce = s32[32]{0:T(128)S(1)} all-reduce(s32[32]{0:T(128)S(1)} %dynamic-update-slice), channel_id=1, replica_groups=mesh['group'=2,'ctx'=16] {'ctx'}, use_global_device_ids=true, to_apply=%add | all-reduce | flops 32 | bytes 256
  106.1 0.1 iota_add_fusion.1
  106.2 0.7 slice_reduce_fusion.1
  106.9 0.7 iota_add_fusion
  109.9 24.0 %all-gather.8.cloned.1.call-done = bf16[2048,512]{1,0:T(8,128)(2,1)} async-done(((bf16[128,512]{1,0:T(8,128)(2,1)}), bf16[2048,512]{1,0:T(8,128)(2,1)}) %all-gather.8.cloned.1.call-update) | async-done | bytes 2097168 | tf_op jit(solution)/shard_map/all_gather | solution.py:59
  133.9 4.0 %reshape.101 = bf16[2048,4,128]{2,1,0:T(4,128)(2,1)} reshape(bf16[2048,512]{1,0:T(8,128)(2,1)} %all-gather.8.cloned.1.call-done) | data formatting | bytes 4194304 | tf_op jit(solution)/shard_map/reshape | solution.py:59
  137.9 38.2 %all-gather.4.cloned.1.call-done = bf16[2048,512]{0,1:T(8,128)(2,1)} async-done(((bf16[128,512]{0,1:T(8,128)(2,1)}), bf16[2048,512]{0,1:T(8,128)(2,1)}) %all-gather.4.cloned.1.call-update) | async-done | bytes 2097168 | tf_op jit(solution)/shard_map/all_gather | solution.py:55
  176.1 14.9 %conditional.2 = (f32[4,8,64]{2,1,0:T(8,128)S(1)}, f32[4,8,64,128]{3,2,1,0:T(8,128)S(1)}) conditional(s32[]{:T(128)} %convert_element_type.36, () %tuple.21, (s32[1,64]{1,0:T(1,128)S(1)}, s32[32,64]{1,0:T(8,128)S(1)}, bf16[128,4096]{1,0:T(8,128)(2,1)}, bf16[2048,4,128]{0,2,1:T(8,128)(2,1)}, bf16[2048,4,128]{2,1,0:T(4,128)(2,1)}) %tuple.46), branch_computations={%region_2.0_spmd, %region_3.6_spmd} | conditional | flops 2202138624 | bytes 67182896 | solution.py:88
  176.1 0.1 ge.34
  176.2 0.1 broadcast_compare_fusion
  176.3 1.2 slice_bitcast_fusion
  177.5 0.1 copy.33
  177.6 4.4 %fusion = (f32[4,8,64]{2,1,0:T(8,128)S(1)}, f32[4,2048,64,8]{1,2,3,0:T(8,128)S(1)}) fusion(pred[64,2048]{1,0:T(8,128)(4,1)S(1)} %broadcast_compare_fusion, bf16[64,4,8,128]{3,2,1,0:T(8,128)(2,1)S(1)} %bitcast.69, bf16[2048,4,128]{0,2,1:T(8,128)(2,1)} %get-tuple-element.62), kind=kOutput, calls=%fused_computation.2 | convolution fusion | flops 1086322688 | bytes 19537920 | tf_op jit(solution)/shard_map/cond/branch_1_fun/tkgd,skd->kgts/dot_general | solution.py:69
  182.1 0.0 copy-done.1
  182.1 3.8 %fusion.3 = f32[4,8,64,128]{3,2,1,0:T(8,128)S(1)} fusion(f32[4,2048,64,8]{1,2,3,0:T(8,128)S(1)} %get-tuple-element.72, f32[4,8,64]{2,1,0:T(8,128)S(1)} %broadcast_maximum_fusion, pred[64,2048]{1,0:T(8,128)(4,1)S(1)} %broadcast_compare_fusion, bf16[2048,4,128,1]{2,1,0,3:T(4,128)(2,1)S(1)} %bitcast.71), kind=kOutput, calls=%fused_computation.5 | convolution fusion | flops 1094713344 | bytes 20062208 | tf_op jit(solution)/shard_map/cond/branch_1_fun/kgts,skd->kgtd/dot_general | solution.py:77
  185.9 5.1 %fusion.2 = f32[4,8,64]{2,1,0:T(8,128)S(1)} fusion(f32[4,2048,64,8]{1,2,3,0:T(8,128)S(1)} %get-tuple-element.72, f32[4,8,64]{2,1,0:T(8,128)S(1)} %broadcast_maximum_fusion, pred[64,2048]{1,0:T(8,128)(4,1)S(1)} %broadcast_compare_fusion), kind=kLoop, calls=%fused_computation.4 | loop fusion | flops 20969472 | bytes 16924672 | tf_op jit(solution)/shard_map/cond/branch_1_fun/reduce_sum | solution.py:76
  191.1 0.3 fusion.28
  191.4 1.1 copy.17
  192.5 14.9 %conditional.3 = (f32[4,8,64]{2,1,0:T(8,128)S(1)}, f32[4,8,64,128]{3,2,1,0:T(8,128)S(1)}) conditional(s32[]{:T(128)} %convert_element_type.42, () %tuple.23, (s32[1,64]{1,0:T(1,128)S(1)}, s32[32,64]{1,0:T(8,128)S(1)}, bf16[128,4096]{1,0:T(8,128)(2,1)}, bf16[2048,4,128]{0,2,1:T(8,128)(2,1)}, bf16[2048,4,128]{2,1,0:T(4,128)(2,1)}) %tuple.47), branch_computations={%region_7.8_spmd, %region_8.11_spmd} | conditional | flops 2202138624 | bytes 67182896 | solution.py:88
  192.5 0.1 ge.39
  192.6 0.1 broadcast_compare_fusion.1
  192.8 1.2 slice_bitcast_fusion.1
  194.0 0.1 copy.34
  194.1 4.4 %fusion.13 = (f32[4,8,64]{2,1,0:T(8,128)S(1)}, f32[4,2048,64,8]{1,2,3,0:T(8,128)S(1)}) fusion(pred[64,2048]{1,0:T(8,128)(4,1)S(1)} %broadcast_compare_fusion.1, bf16[64,4,8,128]{3,2,1,0:T(8,128)(2,1)S(1)} %bitcast.70, bf16[2048,4,128]{0,2,1:T(8,128)(2,1)} %get-tuple-element.67), kind=kOutput, calls=%fused_computation.19 | convolution fusion | flops 1086322688 | bytes 19537920 | tf_op jit(solution)/shard_map/cond/branch_1_fun/tkgd,skd->kgts/dot_general | solution.py:69
  198.5 3.8 %fusion.16 = f32[4,8,64,128]{3,2,1,0:T(8,128)S(1)} fusion(f32[4,2048,64,8]{1,2,3,0:T(8,128)S(1)} %get-tuple-element.74, f32[4,8,64]{2,1,0:T(8,128)S(1)} %broadcast_maximum_fusion.1, pred[64,2048]{1,0:T(8,128)(4,1)S(1)} %broadcast_compare_fusion.1, bf16[2048,4,128,1]{2,1,0,3:T(4,128)(2,1)S(1)} %bitcast.72), kind=kOutput, calls=%fused_computation.22 | convolution fusion | flops 1094713344 | bytes 20062208 | tf_op jit(solution)/shard_map/cond/branch_1_fun/kgts,skd->kgtd/dot_general | solution.py:77
  202.4 5.1 %fusion.15 = f32[4,8,64]{2,1,0:T(8,128)S(1)} fusion(f32[4,2048,64,8]{1,2,3,0:T(8,128)S(1)} %get-tuple-element.74, f32[4,8,64]{2,1,0:T(8,128)S(1)} %broadcast_maximum_fusion.1, pred[64,2048]{1,0:T(8,128)(4,1)S(1)} %broadcast_compare_fusion.1), kind=kLoop, calls=%fused_computation.21 | loop fusion | flops 20969472 | bytes 16924672 | tf_op jit(solution)/shard_map/cond/branch_1_fun/reduce_sum | solution.py:76
  207.5 0.3 fusion.29
  207.8 0.3 copy.20
  208.2 1.4 copy_bitcast_fusion
  209.6 1.1 pad_maximum_fusion
  (12 shorter events, 0.0 us)
Async XLA Ops:
  6.5 80.6 %copy-start = (bf16[128,8192]{1,0:T(8,128)(2,1)S(1)}, bf16[128,8192]{1,0:T(8,128)(2,1)}, u32[]{:S(2)}) copy-start(bf16[128,8192]{1,0:T(8,128)(2,1)} %param.11) | copy-start | bytes 6291460
  6.5 88.5 %copy-start.6 = (u32[32]{0:T(128)S(1)}, u32[32]{0:T(128)}, u32[]{:S(2)}) copy-start(u32[32]{0:T(128)} %constant.9) | copy-start | bytes 388
  6.5 85.3 %copy-start.3 = (bf16[8192,64]{0,1:T(8,128)(2,1)S(1)}, bf16[8192,64]{0,1:T(8,128)(2,1)}, u32[]{:S(2)}) copy-start(bf16[8192,64]{0,1:T(8,128)(2,1)} %param.15) | copy-start | bytes 3145732
  6.5 87.7 %copy-start.4 = (bf16[128,512]{1,0:T(8,128)(2,1)S(1)}, bf16[128,512]{1,0:T(8,128)(2,1)}, u32[]{:S(2)}) copy-start(bf16[128,512]{1,0:T(8,128)(2,1)} %param.13) | copy-start | bytes 393220
  6.5 89.7 %copy-start.5 = (s32[2]{0:T(128)S(1)}, s32[2]{0:T(128)}, u32[]{:S(2)}) copy-start(s32[2]{0:T(128)} %param.17) | copy-start | bytes 28
  6.5 80.6 %all-gather.6.cloned.1.call-start = ((), (), s32[]{:S(2)}) async-start(), calls=%async_computation.1 | async-start | bytes 8912896 | tf_op jit(solution)/shard_map/all_gather | solution.py:28
  7.3 126.7 %all-gather.8.cloned.1.call-start = ((), (), s32[]{:S(2)}) async-start(), calls=%async_computation.2 | async-start | bytes 2228224 | tf_op jit(solution)/shard_map/all_gather | solution.py:59
  94.2 81.9 %all-gather.4.cloned.1.call-start = ((), (), s32[]{:S(2)}) async-start(), calls=%async_computation | async-start | bytes 2228224 | tf_op jit(solution)/shard_map/all_gather | solution.py:55
  176.2 5.9 %copy-start.1 = (bf16[2048,4,128]{2,1,0:T(4,128)(2,1)S(1)}, bf16[2048,4,128]{2,1,0:T(4,128)(2,1)}, u32[]{:S(2)}) copy-start(bf16[2048,4,128]{2,1,0:T(4,128)(2,1)} %get-tuple-element.63) | copy-start | bytes 6291460 | tf_op jit(solution)/shard_map/cond
  192.6 5.9 %copy-start.2 = (bf16[2048,4,128]{2,1,0:T(4,128)(2,1)S(1)}, bf16[2048,4,128]{2,1,0:T(4,128)(2,1)}, u32[]{:S(2)}) copy-start(bf16[2048,4,128]{2,1,0:T(4,128)(2,1)} %get-tuple-element.68) | copy-start | bytes 6291460 | tf_op jit(solution)/shard_map/cond
Sparse Core Ops, SparseCore 0:
  9.5 77.5 all-gather.5
  94.3 39.5 all-gather.7
  136.1 39.9 all-gather.3
where the time goes:
time: 218 us; the launch traced here: 217 us
  waiting for transfers between devices  143 us (66%)
  matrix products  23.5 us (11%)
  between operations  16.1 us (7%)
  other arithmetic  13.7 us (6%)
  local copies, waits for them, and re-layouts  11.2 us (5%)
  blocking collectives  9.61 us (4%)
    all_gather x1, waiting for transfers between devices, shards(): lax.all_gather(value_frozen_matrix, 'ctx', axis=0, tiled=True)  79.8 us
    all_gather x1, waiting for transfers between devices, shards(): key_piece = lax.all_gather(keys, 'ctx', axis=0, tiled=True)  38.2 us
    all_gather x1, waiting for transfers between devices, shards(): lax.all_gather(value_output, 'ctx', axis=0, tiled=True)  24 us
    reduce_sum x2, other arithmetic, update(): total = jnp.sum(weights, axis=-1)  10.2 us
    unnamed x1, blocking collectives  9.61 us
    dot_general x2, matrix products, update(): jnp.einsum('tkgd,skd->kgts', q_part, key_three, preferred_element_type=jn...  8.88 us
    dot_general x2, matrix products, update(): jnp.einsum('kgts,skd->kgtd', weights.astype(jnp.bfloat16), value_three, p...  7.67 us
    dot_general x1, matrix products, shards(): jnp.dot(normed_hidden, lax.all_gather(value_frozen_matrix, 'ctx', axis=0,...  4.63 us
  transfers between devices with their start and end apart: 3, of which 3 were waited for; matrix products, arithmetic and copies ran while one was open for 3% of the time, Pallas kernels for 0%

commit v1 on v0

--- a/solution.py
+++ b/solution.py
@@ -1,6 +1,10 @@
+import functools
+
 import jax
 import jax.numpy as jnp
 from jax import lax
+from jax.experimental import pallas as pl
+from jax.experimental.pallas import tpu as pltpu
 from jax.sharding import PartitionSpec as P
 
 QH = 32
@@ -96,6 +100,283 @@
     return jnp.concatenate(outputs, axis=0)
 
 
+NZ = 4
+NC = 2
+G = QH // KVH
+NSLOT = 4 * NZ
+HU = 2
+
+
+def fused_kernel(
+    slot_ref, hid_ref, q_ref, k_ref, w_ref, down_ref, up_ref, out_ref,
+    kbuf, vbuf, wbuf, hall, psend, precv, wts, recip, bias,
+    k_ss, k_rs, w_ss, w_rs, h_ss, h_rs, p_ss, p_rs, v_ss, v_rs,
+):
+    f32, bf16 = jnp.float32, jnp.bfloat16
+    x = lax.axis_index("group")
+    me = lax.axis_index("ctx")
+    z, y, c = me // 4, (me // 2) % 2, me % 2
+    tokens = k_ref.shape[0]
+    half = w_ref.shape[0] // 2
+    cols = w_ref.shape[1] // NC
+    hpc = QH // NC
+
+    def at(gx, zz, yy, cc):
+        return (gx, zz * 4 + yy * 2 + cc)
+
+    z_peer = {d: at(x, (z + d) % NZ, y, c) for d in range(1, NZ)}
+    y_peer = at(x, z, 1 - y, c)
+    c_peer = at(x, z, y, 1 - c)
+    p_peer = [None, at(x, z, y, 1 - c), at(1 - x, z, y, c), at(1 - x, z, y, 1 - c)]
+    started = []
+
+    def remote(src, dst, ss, rs, peer):
+        return pltpu.make_async_remote_copy(
+            src_ref=src, dst_ref=dst, send_sem=ss, recv_sem=rs,
+            device_id=peer, device_id_type=pl.DeviceIdType.MESH,
+        )
+
+    def go(copy):
+        copy.start()
+        started.append(copy)
+        return copy
+
+    b0 = slot_ref[0].astype(f32)
+    b1 = slot_ref[1].astype(f32)
+    kbuf[0, :tokens, :] = k_ref[...]
+    lane = lax.broadcasted_iota(jnp.int32, (16, k_ref.shape[1]), 1) % tokens
+    kbuf[0, tokens:, :] = jnp.where(lane < BLK, b0, b1).astype(bf16)
+
+    barrier = pltpu.get_barrier_semaphore()
+    peers = list(z_peer.values()) + [y_peer] + p_peer[1:]
+    for peer in peers:
+        pl.semaphore_signal(barrier, inc=1, device_id=peer, device_id_type=pl.DeviceIdType.MESH)
+    pl.semaphore_wait(barrier, len(peers))
+
+    def gather(src0, view, ss, rs, pair=True):
+        zc = {d: remote(src0, view(NZ - d), ss(d - 1), rs(d - 1), z_peer[d]) for d in range(1, NZ)}
+        yc = {}
+        cc = {}
+        for j in range(NZ):
+            yc[j] = remote(src0 if j == 0 else view(j), view(4 + j), ss(3 + j), rs(3 + j), y_peer)
+        for j in range(2 * NZ if pair else 0):
+            cc[j] = remote(src0 if j == 0 else view(j), view(8 + j), ss(7 + j), rs(7 + j), c_peer)
+        return zc, yc, cc
+
+    kz, ky, kc = gather(kbuf.at[0], lambda s: kbuf.at[s], lambda i: k_ss.at[i], lambda i: k_rs.at[i])
+    for d in range(1, NZ):
+        go(kz[d])
+    go(ky[0])
+    go(kc[0])
+
+    def column(j, cc, xx):
+        dz, dy = j % NZ, j // NZ
+        block = at(0, (z + dz) % NZ, (y + dy) % 2, cc)[1]
+        return pl.multiple_of(block * (2 * half) + xx * half, half)
+
+    hc = {}
+    for p in (2, 3, 1):
+        px, pc = (x, 1 - x)[p // 2], (c, 1 - c)[p % 2]
+        for j in range(2 * NZ):
+            hc[p, j] = go(remote(
+                hid_ref.at[:, pl.ds(column(j, pc, px), half)],
+                hall.at[pl.ds(p * tokens, tokens), pl.ds(j * half, half)],
+                h_ss.at[p - 1, j], h_rs.at[p - 1, j], p_peer[p],
+            ))
+
+    row0 = pl.multiple_of(x * half, half)
+    wz, wy = [], []
+    for ch in range(NC):
+        wbuf[ch, :half, :] = w_ref[pl.ds(row0, half), ch * cols:(ch + 1) * cols]
+        zc, yc, _ = gather(
+            wbuf.at[ch, pl.ds(0, half)],
+            lambda s, ch=ch: wbuf.at[ch, pl.ds((s % 8) * half, half)],
+            lambda i, ch=ch: w_ss.at[ch, i], lambda i, ch=ch: w_rs.at[ch, i], pair=False,
+        )
+        wz.append(zc)
+        wy.append(yc)
+
+    def w_send(ch):
+        for d in range(1, NZ):
+            go(wz[ch][d])
+        go(wy[ch][0])
+
+    def z_forward(zc, yc, cc=None):
+        for d in (1, 3, 2):
+            zc[d].wait_recv()
+            go(yc[NZ - d])
+            if cc is not None:
+                go(cc[NZ - d])
+
+    def y_forward(yc, cc):
+        for j in range(NZ):
+            yc[j].wait_recv()
+            go(cc[NZ + j])
+
+    w_send(0)
+    low = jnp.dot(hid_ref[...], down_ref[...], preferred_element_type=f32).astype(bf16)
+    for j in range(2 * NZ):
+        hall[:tokens, j * half:(j + 1) * half] = hid_ref[:, pl.ds(column(j, c, x), half)]
+    adapter = 0.5 * jnp.dot(low, up_ref[...], preferred_element_type=f32)
+
+    z_forward(kz, ky, kc)
+    y_forward(ky, kc)
+    z_forward(wz[0], wy[0])
+    w_send(1)
+    for j in range(2 * NZ):
+        kc[j].wait_recv()
+
+    row = lax.broadcasted_iota(jnp.int32, (tokens, tokens), 0)
+    col = lax.broadcasted_iota(jnp.int32, (tokens, tokens), 1)
+    q_pos = jnp.where(row < BLK, b0, b1) * BLK + (row % BLK).astype(f32)
+    for s in range(NSLOT):
+        blocks = kbuf[s, tokens:, :tokens].astype(f32)[0:1]
+        k_pos = blocks * BLK + (col % BLK).astype(f32)
+        bias[:, s * tokens:(s + 1) * tokens] = jnp.where(q_pos >= k_pos, 0.0, -1e30)
+
+    rate = 1.4426950408889634 / HD**0.5
+    count = NSLOT * tokens
+
+    def softmax(first, last):
+        for g in range(KVH):
+            lo, hi = max(first, g * G), min(last, (g + 1) * G)
+            if lo >= hi:
+                continue
+
+            @pl.loop(lo // HU, hi // HU)
+            def _(u, g=g):
+                keys = kbuf[:, :tokens, g * HD:(g + 1) * HD].reshape(count, HD)
+                q = jnp.concatenate(
+                    [q_ref[:, pl.ds(pl.multiple_of((u * HU + i) * HD, HD), HD)] for i in range(HU)], axis=0
+                )
+                s = lax.dot_general(q, keys, (((1,), (1,)), ((), ())), preferred_element_type=f32)
+                s = s.reshape(HU, tokens, count) + bias[...][None]
+                top = jnp.max(s, axis=-1, keepdims=True)
+                e = jnp.exp2((s - top) * rate)
+                total = jnp.sum(e, axis=-1, keepdims=True)
+                wts[pl.ds(u * HU, HU)] = e.astype(bf16)
+                recip[pl.ds(u * HU, HU)] = jnp.broadcast_to(1.0 / total, (HU, tokens, HD))
+
+    pc = {}
+    vz, vy, vc = [], [], []
+    for ch in range(NC):
+        zc, yc, cc = gather(
+            vbuf.at[0, :, pl.ds(ch * cols, cols)],
+            lambda s, ch=ch: vbuf.at[s, :, pl.ds(ch * cols, cols)],
+            lambda i, ch=ch: v_ss.at[ch, i], lambda i, ch=ch: v_rs.at[ch, i],
+        )
+        vz.append(zc)
+        vy.append(yc)
+        vc.append(cc)
+    own = {}
+
+    def partial(ch):
+        acc = jnp.dot(hall[...], wbuf[ch], preferred_element_type=f32)
+        for p in (3, 2, 1):
+            psend[ch, p - 1] = acc[p * tokens:(p + 1) * tokens].astype(bf16)
+            pc[ch, p] = go(remote(
+                psend.at[ch, p - 1], precv.at[ch, p - 1], p_ss.at[ch, p - 1], p_rs.at[ch, p - 1], p_peer[p]
+            ))
+        own[ch] = acc[:tokens] + adapter[:, ch * cols:(ch + 1) * cols]
+
+    def values(ch):
+        acc = own[ch]
+        for p in (1, 2, 3):
+            pc[ch, p].wait_recv()
+            acc = acc + precv[ch, p - 1].astype(f32)
+        vbuf[0, :, ch * cols:(ch + 1) * cols] = acc.astype(bf16)
+        for d in range(1, NZ):
+            go(vz[ch][d])
+        go(vy[ch][0])
+        go(vc[ch][0])
+
+    def attend(ch):
+        for g in range(ch * KVH // NC, (ch + 1) * KVH // NC):
+            @pl.loop(g * G // HU, (g + 1) * G // HU)
+            def _(u, g=g):
+                v = vbuf[:, :, g * HD:(g + 1) * HD].reshape(count, HD)
+                w = wts[pl.ds(u * HU, HU)].reshape(HU * tokens, count)
+                o = jnp.dot(w, v, preferred_element_type=f32)
+                for i in range(HU):
+                    r = o[i * tokens:(i + 1) * tokens] * recip[u * HU + i]
+                    out_ref[:, pl.ds(pl.multiple_of((u * HU + i) * HD, HD), HD)] = r.astype(bf16)
+
+    softmax(0, 6)
+    z_forward(wz[1], wy[1])
+    softmax(6, 12)
+    for copy in hc.values():
+        copy.wait_recv()
+    for j in range(NZ):
+        wy[0][j].wait_recv()
+    partial(0)
+    softmax(12, 18)
+    values(0)
+    for j in range(NZ):
+        wy[1][j].wait_recv()
+    partial(1)
+    softmax(18, 24)
+    z_forward(vz[0], vy[0], vc[0])
+    values(1)
+    softmax(24, 32)
+    y_forward(vy[0], vc[0])
+    z_forward(vz[1], vy[1], vc[1])
+    for j in range(2 * NZ):
+        vc[0][j].wait_recv()
+    attend(0)
+    y_forward(vy[1], vc[1])
+    for j in range(2 * NZ):
+        vc[1][j].wait_recv()
+    attend(1)
+    for copy in started:
+        copy.wait_send()
+
+
+def fused_shards(
+    normed_hidden,
+    queries,
+    keys,
+    value_frozen_matrix,
+    adapter_down_weight,
+    adapter_up_weight,
+    block_slot_index,
+):
+    tokens, width = keys.shape
+    rows = value_frozen_matrix.shape[0]
+    cols = width // NC
+    bf16 = jnp.bfloat16
+    vmem = pl.BlockSpec(memory_space=pltpu.VMEM)
+    dma = pltpu.SemaphoreType.DMA
+    return pl.pallas_call(
+        fused_kernel,
+        out_shape=jax.ShapeDtypeStruct(queries.shape, bf16),
+        in_specs=[pl.BlockSpec(memory_space=pltpu.SMEM)] + [vmem] * 6,
+        out_specs=vmem,
+        scratch_shapes=[
+            pltpu.VMEM((NSLOT, tokens + 16, width), bf16),
+            pltpu.VMEM((NSLOT, tokens, width), bf16),
+            pltpu.VMEM((NC, 4 * rows, cols), bf16),
+            pltpu.VMEM((4 * tokens, 4 * rows), bf16),
+            pltpu.VMEM((NC, 3, tokens, cols), bf16),
+            pltpu.VMEM((NC, 3, tokens, cols), bf16),
+            pltpu.VMEM((QH, tokens, NSLOT * tokens), bf16),
+            pltpu.VMEM((QH, tokens, HD), jnp.float32),
+            pltpu.VMEM((tokens, NSLOT * tokens), jnp.float32),
+            dma((15,)), dma((15,)),
+            dma((NC, 7)), dma((NC, 7)),
+            dma((3, 8)), dma((3, 8)),
+            dma((NC, 3)), dma((NC, 3)),
+            dma((NC, 15)), dma((NC, 15)),
+        ],
+        compiler_params=pltpu.CompilerParams(
+            collective_id=0, has_side_effects=True, vmem_limit_bytes=56 * 2**20
+        ),
+        cost_estimate=pl.CostEstimate(flops=6 * 10**9, bytes_accessed=8 * 10**6, transcendentals=8 * 10**6),
+    )(
+        block_slot_index, normed_hidden, queries, keys,
+        value_frozen_matrix, adapter_down_weight, adapter_up_weight,
+    )
+
+
 def solution(mesh):
     in_specs = (
         P(("group", "ctx"), None),
@@ -107,4 +388,5 @@
         P(("group", "ctx")),
     )
     out_specs = P(("group", "ctx"), None)
-    return jax.shard_map(shards, mesh=mesh, in_specs=in_specs, out_specs=out_specs, check_vma=False)
+    body = fused_shards if mesh.shape["ctx"] == 4 * NZ and mesh.shape["group"] == 2 else shards
+    return jax.shard_map(body, mesh=mesh, in_specs=in_specs, out_specs=out_specs, check_vma=False)

time: 218 us -> 81.9 us (0.38)
  waiting for transfers between devices: 143 us -> 0 us
  Pallas kernels: 0 us -> 75.8 us
  matrix products: 23.5 us -> 0 us
  between operations: 16.1 us -> 0.01 us
  other arithmetic: 13.7 us -> 0 us
  blocking collectives: 9.61 us -> 0 us
  local copies, waits for them, and re-layouts: 11.2 us -> 5.06 us
    all_gather x3 -> x0, waiting for transfers between devices: 142 us -> none  [the longest x1 79.8 us: shards(): lax.all_gather(value_frozen_matrix, 'ctx', axis=0, tiled=True)]
    pallas_call x0 -> x1, Pallas kernels: none -> 75.8 us  [fused_shards(): pl.pallas_call(fused_kernel, out_shape=jax.ShapeDtypeStruct(queries.shape...]
    dot_general x6 -> x0, matrix products: 23.5 us -> none  [the longest x2 8.88 us: update(): jnp.einsum('tkgd,skd->kgts', q_part, key_three, preferred_element_type=jn...]
    reduce_sum x2 -> x0, other arithmetic: 10.2 us -> none  [update(): total = jnp.sum(weights, axis=-1)]
    unnamed x1 -> x0, blocking collectives: 9.61 us -> none
    reshape x1 -> x0, local copies, waits for them, and re-layouts: 3.96 us -> none  [shards(): lax.all_gather(value_output, 'ctx', axis=0, tiled=True)]
    unnamed x14 -> x2, local copies, waits for them, and re-layouts: 1.6 us -> 5.06 us
    convert_element_type x3 -> x0, local copies, waits for them, and re-layouts: 2.92 us -> none  [shards(): jnp.transpose(result, (2, 0, 1, 3)).reshape(BLK, QH * HD)]
  transfers between devices with their start and end apart: 3 -> 0, of which waited for: 3 -> 0; matrix products, arithmetic and copies ran while one was open for 3% -> 0% of each run, Pallas kernels for 0% -> 0%
where the time goes in v1:
time: 81.9 us; the launch traced here: 80.9 us
  Pallas kernels  75.8 us (93%)
  local copies, waits for them, and re-layouts  5.06 us (6%)
    pallas_call x1, Pallas kernels, fused_shards(): pl.pallas_call(fused_kernel, out_shape=jax.ShapeDtypeStruct(queries.shape...  75.8 us
    unnamed x2, local copies, waits for them, and re-layouts  5.06 us

profile of v1, /device:TPU:0, one launch (start us, length us, event | category | flops | bytes accessed | tf_op | source)
XLA Modules:
  0.0 80.9 jit_solution(1420153238203016861)
XLA Ops:
  0.0 2.8 %copy.8.down_ref = bf16[8192,64]{1,0:T(8,128)(2,1)} copy(bf16[8192,64]{0,1:T(8,128)(2,1)} %param.11) | data formatting | bytes 2097152 | tf_op args[4]
  2.8 75.8 %shard_map.73 = bf16[128,4096]{1,0:T(8,128)(2,1)} custom-call(s32[2]{0:T(128)} %slot_ref.1, bf16[128,8192]{1,0:T(8,128)(2,1)} %hid_ref.1, bf16[128,4096]{1,0:T(8,128)(2,1)} %q_ref.1, bf16[128,512]{1,0:T(8,128)(2,1)} %k_ref.1, bf16[512,512]{1,0:T(8,128)(2,1)} %w_ref.1, bf16[8192,64]{1,0:T(8,128)(2,1)} %copy.8.down_ref, bf16[64,512]{1,0:T(8,128)(2,1)} %up_ref.1), custom_call_target="tpu_custom_call" | custom-call | flops 6000000000 | bytes 8000000 | tf_op jit(solution)/shard_map/pallas_call | solution.py:349
  78.6 2.3 %copy.10 = bf16[128,4096]{1,0:T(8,128)(2,1)} copy(bf16[128,4096]{1,0:T(8,128)(2,1)} %shard_map.73) | data formatting | bytes 2097152

commit v2 on v1

--- a/solution.py
+++ b/solution.py
@@ -101,15 +101,17 @@
 
 
 NZ = 4
-NC = 2
+NC = 4
+AHEAD = 4
 G = QH // KVH
 NSLOT = 4 * NZ
 HU = 2
+HA = 4
 
 
 def fused_kernel(
-    slot_ref, hid_ref, q_ref, k_ref, w_ref, down_ref, up_ref, out_ref,
-    kbuf, vbuf, wbuf, hall, psend, precv, wts, recip, bias,
+    slot_ref, hid_hbm, q_hbm, k_ref, w_ref, down_hbm, up_ref, out_ref,
+    kbuf, vbuf, wbuf, hall, psend, precv, wts, recip, bias, hid_ref, q_ref, down_ref, load_sem,
     k_ss, k_rs, w_ss, w_rs, h_ss, h_rs, p_ss, p_rs, v_ss, v_rs,
 ):
     f32, bf16 = jnp.float32, jnp.bfloat16
@@ -141,11 +143,16 @@
         started.append(copy)
         return copy
 
+    loads = [
+        pltpu.make_async_copy(src, dst, load_sem.at[i])
+        for i, (src, dst) in enumerate(((down_hbm, down_ref), (hid_hbm, hid_ref), (q_hbm, q_ref)))
+    ]
     b0 = slot_ref[0].astype(f32)
     b1 = slot_ref[1].astype(f32)
-    kbuf[0, :tokens, :] = k_ref[...]
-    lane = lax.broadcasted_iota(jnp.int32, (16, k_ref.shape[1]), 1) % tokens
-    kbuf[0, tokens:, :] = jnp.where(lane < BLK, b0, b1).astype(bf16)
+    for g in range(KVH):
+        kbuf[g, 0, :tokens, :] = k_ref[:, g * HD:(g + 1) * HD]
+    lane = lax.broadcasted_iota(jnp.int32, (16, HD), 1)
+    kbuf[0, 0, tokens:, :] = jnp.where(lane < BLK, b0, b1).astype(bf16)
 
     barrier = pltpu.get_barrier_semaphore()
     peers = list(z_peer.values()) + [y_peer] + p_peer[1:]
@@ -163,11 +170,43 @@
             cc[j] = remote(src0 if j == 0 else view(j), view(8 + j), ss(7 + j), rs(7 + j), c_peer)
         return zc, yc, cc
 
-    kz, ky, kc = gather(kbuf.at[0], lambda s: kbuf.at[s], lambda i: k_ss.at[i], lambda i: k_rs.at[i])
-    for d in range(1, NZ):
-        go(kz[d])
-    go(ky[0])
-    go(kc[0])
+    queue, front = [], [0, 0]
+
+    def enqueue(zc, yc, cc):
+        for i, d in enumerate((1, 3, 2)):
+            first = ([yc[0]] + ([cc[0]] if cc else [])) if i == 0 else []
+            queue.append((zc[d], yc[NZ - d], cc.get(NZ - d), first))
+
+    def launch(n):
+        for item in queue[front[0]:front[0] + n]:
+            for copy in item[3]:
+                go(copy)
+            go(item[0])
+        front[0] = min(front[0] + n, len(queue))
+
+    def pump(n):
+        for item in queue[front[1]:front[1] + n]:
+            item[0].wait_recv()
+            go(item[1])
+            if item[2] is not None:
+                go(item[2])
+            launch(1)
+        front[1] += n
+
+    kz, ky, kc = [], [], []
+    for g in range(KVH):
+        sent = pl.ds(0, tokens + 16 if g == 0 else tokens)
+        zc, yc, cc = gather(
+            kbuf.at[g, 0, sent],
+            lambda s, g=g, sent=sent: kbuf.at[g, s, sent],
+            lambda i, g=g: k_ss.at[g, i], lambda i, g=g: k_rs.at[g, i],
+        )
+        kz.append(zc)
+        ky.append(yc)
+        kc.append(cc)
+    enqueue(kz[0], ky[0], kc[0])
+    enqueue(kz[1], ky[1], kc[1])
+    launch(3)
 
     def column(j, cc, xx):
         dz, dy = j % NZ, j // NZ
@@ -179,13 +218,13 @@
         px, pc = (x, 1 - x)[p // 2], (c, 1 - c)[p % 2]
         for j in range(2 * NZ):
             hc[p, j] = go(remote(
-                hid_ref.at[:, pl.ds(column(j, pc, px), half)],
+                hid_hbm.at[:, pl.ds(column(j, pc, px), half)],
                 hall.at[pl.ds(p * tokens, tokens), pl.ds(j * half, half)],
                 h_ss.at[p - 1, j], h_rs.at[p - 1, j], p_peer[p],
             ))
 
     row0 = pl.multiple_of(x * half, half)
-    wz, wy = [], []
+    wy = []
     for ch in range(NC):
         wbuf[ch, :half, :] = w_ref[pl.ds(row0, half), ch * cols:(ch + 1) * cols]
         zc, yc, _ = gather(
@@ -193,13 +232,12 @@
             lambda s, ch=ch: wbuf.at[ch, pl.ds((s % 8) * half, half)],
             lambda i, ch=ch: w_ss.at[ch, i], lambda i, ch=ch: w_rs.at[ch, i], pair=False,
         )
-        wz.append(zc)
+        enqueue(zc, yc, {})
         wy.append(yc)
-
-    def w_send(ch):
-        for d in range(1, NZ):
-            go(wz[ch][d])
-        go(wy[ch][0])
+        if ch >= 2:
+            enqueue(kz[ch], ky[ch], kc[ch])
+
+    launch(AHEAD - 3)
 
     def z_forward(zc, yc, cc=None):
         for d in (1, 3, 2):
@@ -213,24 +251,32 @@
             yc[j].wait_recv()
             go(cc[NZ + j])
 
-    w_send(0)
-    low = jnp.dot(hid_ref[...], down_ref[...], preferred_element_type=f32).astype(bf16)
+    for copy in loads:
+        copy.start()
+    pump(3)
+    loads[1].wait()
     for j in range(2 * NZ):
         hall[:tokens, j * half:(j + 1) * half] = hid_ref[:, pl.ds(column(j, c, x), half)]
+    pump(3)
+    y_forward(ky[0], kc[0])
+    loads[0].wait()
+    low = lax.dot_general(
+        hid_ref[...], down_ref[...], (((1,), (1,)), ((), ())), preferred_element_type=f32
+    ).astype(bf16)
     adapter = 0.5 * jnp.dot(low, up_ref[...], preferred_element_type=f32)
 
-    z_forward(kz, ky, kc)
-    y_forward(ky, kc)
-    z_forward(wz[0], wy[0])
-    w_send(1)
-    for j in range(2 * NZ):
-        kc[j].wait_recv()
+    def k_wait(g):
+        for j in range(2 * NZ):
+            kc[g][j].wait_recv()
+
+    k_wait(0)
+    pump(1)
 
     row = lax.broadcasted_iota(jnp.int32, (tokens, tokens), 0)
     col = lax.broadcasted_iota(jnp.int32, (tokens, tokens), 1)
     q_pos = jnp.where(row < BLK, b0, b1) * BLK + (row % BLK).astype(f32)
     for s in range(NSLOT):
-        blocks = kbuf[s, tokens:, :tokens].astype(f32)[0:1]
+        blocks = kbuf[0, s, tokens:, :].astype(f32)[0:1]
         k_pos = blocks * BLK + (col % BLK).astype(f32)
         bias[:, s * tokens:(s + 1) * tokens] = jnp.where(q_pos >= k_pos, 0.0, -1e30)
 
@@ -245,7 +291,7 @@
 
             @pl.loop(lo // HU, hi // HU)
             def _(u, g=g):
-                keys = kbuf[:, :tokens, g * HD:(g + 1) * HD].reshape(count, HD)
+                keys = kbuf[g, :, :tokens, :].reshape(count, HD)
                 q = jnp.concatenate(
                     [q_ref[:, pl.ds(pl.multiple_of((u * HU + i) * HD, HD), HD)] for i in range(HU)], axis=0
                 )
@@ -261,8 +307,8 @@
     vz, vy, vc = [], [], []
     for ch in range(NC):
         zc, yc, cc = gather(
-            vbuf.at[0, :, pl.ds(ch * cols, cols)],
-            lambda s, ch=ch: vbuf.at[s, :, pl.ds(ch * cols, cols)],
+            vbuf.at[ch, 0],
+            lambda s, ch=ch: vbuf.at[ch, s],
             lambda i, ch=ch: v_ss.at[ch, i], lambda i, ch=ch: v_rs.at[ch, i],
         )
         vz.append(zc)
@@ -284,7 +330,7 @@
         for p in (1, 2, 3):
             pc[ch, p].wait_recv()
             acc = acc + precv[ch, p - 1].astype(f32)
-        vbuf[0, :, ch * cols:(ch + 1) * cols] = acc.astype(bf16)
+        vbuf[ch, 0] = acc.astype(bf16)
         for d in range(1, NZ):
             go(vz[ch][d])
         go(vy[ch][0])
@@ -292,41 +338,71 @@
 
     def attend(ch):
         for g in range(ch * KVH // NC, (ch + 1) * KVH // NC):
-            @pl.loop(g * G // HU, (g + 1) * G // HU)
+            @pl.loop(g * G // HA, (g + 1) * G // HA)
             def _(u, g=g):
-                v = vbuf[:, :, g * HD:(g + 1) * HD].reshape(count, HD)
-                w = wts[pl.ds(u * HU, HU)].reshape(HU * tokens, count)
+                v = vbuf[ch, :, :, (g * HD) % cols:(g * HD) % cols + HD].reshape(count, HD)
+                w = wts[pl.ds(u * HA, HA)].reshape(HA * tokens, count)
                 o = jnp.dot(w, v, preferred_element_type=f32)
-                for i in range(HU):
-                    r = o[i * tokens:(i + 1) * tokens] * recip[u * HU + i]
-                    out_ref[:, pl.ds(pl.multiple_of((u * HU + i) * HD, HD), HD)] = r.astype(bf16)
-
-    softmax(0, 6)
-    z_forward(wz[1], wy[1])
-    softmax(6, 12)
+                for i in range(HA):
+                    r = o[i * tokens:(i + 1) * tokens] * recip[u * HA + i]
+                    out_ref[:, pl.ds(pl.multiple_of((u * HA + i) * HD, HD), HD)] = r.astype(bf16)
+
+    def w_wait(ch):
+        for j in range(NZ):
+            wy[ch][j].wait_recv()
+
+    def v_wait(ch):
+        for j in range(2 * NZ):
+            vc[ch][j].wait_recv()
+
+    loads[2].wait()
+    softmax(0, 4)
+    pump(2)
+    y_forward(ky[1], kc[1])
+    softmax(4, 8)
+    pump(3)
+    k_wait(1)
+    softmax(8, 12)
+    pump(3)
+    softmax(12, 14)
     for copy in hc.values():
         copy.wait_recv()
-    for j in range(NZ):
-        wy[0][j].wait_recv()
+    w_wait(0)
     partial(0)
-    softmax(12, 18)
+    pump(3)
+    w_wait(1)
+    partial(1)
     values(0)
-    for j in range(NZ):
-        wy[1][j].wait_recv()
-    partial(1)
-    softmax(18, 24)
+    softmax(14, 16)
+    pump(3)
     z_forward(vz[0], vy[0], vc[0])
+    w_wait(2)
+    partial(2)
     values(1)
-    softmax(24, 32)
+    y_forward(ky[2], kc[2])
+    pump(3)
+    z_forward(vz[1], vy[1], vc[1])
+    k_wait(2)
+    softmax(16, 18)
+    w_wait(3)
+    partial(3)
+    values(2)
     y_forward(vy[0], vc[0])
-    z_forward(vz[1], vy[1], vc[1])
-    for j in range(2 * NZ):
-        vc[0][j].wait_recv()
-    attend(0)
+    softmax(18, 22)
+    values(3)
+    z_forward(vz[2], vy[2], vc[2])
+    y_forward(ky[3], kc[3])
     y_forward(vy[1], vc[1])
-    for j in range(2 * NZ):
-        vc[1][j].wait_recv()
-    attend(1)
+    softmax(22, 24)
+    z_forward(vz[3], vy[3], vc[3])
+    k_wait(3)
+    softmax(24, 28)
+    y_forward(vy[2], vc[2])
+    softmax(28, 32)
+    y_forward(vy[3], vc[3])
+    for ch in range(NC):
+        v_wait(ch)
+        attend(ch)
     for copy in started:
         copy.wait_send()
 
@@ -345,15 +421,16 @@
     cols = width // NC
     bf16 = jnp.bfloat16
     vmem = pl.BlockSpec(memory_space=pltpu.VMEM)
+    hbm = pl.BlockSpec(memory_space=pl.ANY)
     dma = pltpu.SemaphoreType.DMA
     return pl.pallas_call(
         fused_kernel,
         out_shape=jax.ShapeDtypeStruct(queries.shape, bf16),
-        in_specs=[pl.BlockSpec(memory_space=pltpu.SMEM)] + [vmem] * 6,
+        in_specs=[pl.BlockSpec(memory_space=pltpu.SMEM), hbm, hbm, vmem, vmem, hbm, vmem],
         out_specs=vmem,
         scratch_shapes=[
-            pltpu.VMEM((NSLOT, tokens + 16, width), bf16),
-            pltpu.VMEM((NSLOT, tokens, width), bf16),
+            pltpu.VMEM((KVH, NSLOT, tokens + 16, HD), bf16),
+            pltpu.VMEM((NC, NSLOT, tokens, cols), bf16),
             pltpu.VMEM((NC, 4 * rows, cols), bf16),
             pltpu.VMEM((4 * tokens, 4 * rows), bf16),
             pltpu.VMEM((NC, 3, tokens, cols), bf16),
@@ -361,7 +438,11 @@
             pltpu.VMEM((QH, tokens, NSLOT * tokens), bf16),
             pltpu.VMEM((QH, tokens, HD), jnp.float32),
             pltpu.VMEM((tokens, NSLOT * tokens), jnp.float32),
-            dma((15,)), dma((15,)),
+            pltpu.VMEM(normed_hidden.shape, bf16),
+            pltpu.VMEM(queries.shape, bf16),
+            pltpu.VMEM(adapter_down_weight.shape[::-1], bf16),
+            dma((3,)),
+            dma((KVH, 15)), dma((KVH, 15)),
             dma((NC, 7)), dma((NC, 7)),
             dma((3, 8)), dma((3, 8)),
             dma((NC, 3)), dma((NC, 3)),
@@ -373,7 +454,7 @@
         cost_estimate=pl.CostEstimate(flops=6 * 10**9, bytes_accessed=8 * 10**6, transcendentals=8 * 10**6),
     )(
         block_slot_index, normed_hidden, queries, keys,
-        value_frozen_matrix, adapter_down_weight, adapter_up_weight,
+        value_frozen_matrix, adapter_down_weight.T, adapter_up_weight,
     )
 
 

time: 81.9 us -> 76.5 us (0.934); the launches traced: 80.9 us -> 76.3 us
  local copies, waits for them, and re-layouts: 5.06 us -> 2.29 us
  Pallas kernels: 75.8 us -> 74 us
    unnamed x2 -> x1, local copies, waits for them, and re-layouts: 5.06 us -> 2.29 us
    pallas_call x1, Pallas kernels: 75.8 us -> 74 us  [fused_shards(): pl.pallas_call(fused_kernel, out_shape=jax.ShapeDtypeStruct(queries.shape...]
where the time goes in v2:
time: 76.5 us; the launch traced here: 76.3 us
  Pallas kernels  74 us (97%)
  local copies, waits for them, and re-layouts  2.29 us (3%)
    pallas_call x1, Pallas kernels, fused_shards(): pl.pallas_call(fused_kernel, out_shape=jax.ShapeDtypeStruct(queries.shape...  74 us
    unnamed x1, local copies, waits for them, and re-layouts  2.29 us

profile of v2, /device:TPU:0, one launch (start us, length us, event | category | flops | bytes accessed | tf_op | source)
XLA Modules:
  0.0 76.3 jit_solution(14848320741460790035)
XLA Ops:
  0.0 74.0 %shard_map.73 = bf16[128,4096]{1,0:T(8,128)(2,1)} custom-call(s32[2]{0:T(128)} %slot_ref.1, bf16[128,8192]{1,0:T(8,128)(2,1)} %hid_hbm.1, bf16[128,4096]{1,0:T(8,128)(2,1)} %q_hbm.1, bf16[128,512]{1,0:T(8,128)(2,1)} %k_ref.1, bf16[512,512]{1,0:T(8,128)(2,1)} %w_ref.1, bf16[64,8192]{1,0:T(8,128)(2,1)} %bitcast.1, bf16[64,512]{1,0:T(8,128)(2,1)} %up_ref.1), custom_call_target="tpu_custom_call" | custom-call | flops 6000000000 | bytes 8000000 | tf_op jit(solution)/shard_map/pallas_call | solution.py:426
  74.0 2.3 %copy.9 = bf16[128,4096]{1,0:T(8,128)(2,1)} copy(bf16[128,4096]{1,0:T(8,128)(2,1)} %shard_map.73) | data formatting | bytes 2097152
